TPU v7x, 32 devices: a whole 2x2x4 slice. The times are simulated.
32 devices in a mesh: ia: 4 (over y, x), ja: 2 (over core), ka: 4 (over z).
Axes of the slice: x: 2, y: 2, z: 4, core: 2. Of those that a mesh axis runs over, the one named last changes fastest.
Arguments:
- tensor: bfloat16 [4096, 32, 4096], P('ia', 'ka', 'ja'), may hold values from -64 to 64
- factor_j: bfloat16 [4096, 128], P('ja'), may hold values from -0.0640625 to 0.0640625
- factor_k: bfloat16 [32, 128], P('ka'), may hold values from -0.72478445 to 0.72478445
Outputs:
- core: float32 [128, 32, 4096], P('ia', 'ka', 'ja')
All inputs are finite; a program needn't handle non-finite values.
Results may differ from a plain program's by a relative error of at most 0.013.
Values may be sent and summed in bfloat16 or wider, within the bound.
A program may use at most 128 MiB of HBM per device.

v0:
```python
import jax
import jax.numpy as jnp
from jax import lax
from jax.sharding import PartitionSpec as P


def local_sketch(tensor, factor_j, factor_k):
    rows, slices, columns = tensor.shape
    mixed = jnp.dot(
        tensor.reshape(rows * slices, columns), factor_j, preferred_element_type=jnp.float32
    )
    mixed = mixed.reshape(rows, slices, factor_j.shape[1])
    return jnp.sum(mixed * factor_k.astype(jnp.float32)[None], axis=1)


def local_gram(basis):
    return jnp.dot(
        basis.T, basis, precision=lax.Precision.HIGHEST, preferred_element_type=jnp.float32
    )


def apply_factor(gram, basis):
    lower = jnp.linalg.cholesky(gram)
    return jax.scipy.linalg.solve_triangular(lower, basis.T, lower=True).T


def shards(tensor, factor_j, factor_k):
    rows, slices, columns = tensor.shape
    partial_value = local_sketch(tensor, factor_j, factor_k)
    basis = lax.psum(partial_value, ("ja", "ka"))
    for sweep in range(2):
        gram = lax.psum(local_gram(basis), "ia")
        basis = apply_factor(gram, basis)
    basis_half = basis.astype(jnp.bfloat16)
    flattened = tensor.reshape(rows, slices * columns)
    width = basis_half.shape[1]
    kept_rows = width // lax.axis_size("ia")
    core = lax.psum_scatter(
        lax.dot_general(
            basis_half, flattened, (((0,), (0,)), ((), ())), preferred_element_type=jnp.float32
        ).astype(jnp.bfloat16),
        "ia",
        scatter_dimension=0,
        tiled=True,
    ).astype(jnp.float32)
    return core.reshape(kept_rows, slices, columns)


def solution(mesh):
    return jax.shard_map(
        shards,
        mesh=mesh,
        in_specs=(P("ia", "ka", "ja"), P("ja", None), P("ka", None)),
        out_specs=P("ia", "ka", "ja"),
        check_vma=False,
    )
```

profile of v0, /device:TPU:0, one launch (start us, length us, event | category | flops | bytes accessed | tf_op | source)
XLA Modules:
  0.0 300.6 jit_solution(7561206188565948169)
XLA Ops:
  6.5 0.7 convert_element_type.11
  7.6 14.7 %fusion.3 = f32[1024,8,128]{2,1,0:T(8,128)S(1)} fusion(bf16[1024,8,2048]{2,1,0:T(8,128)(2,1)} %param.6, bf16[2048,128]{1,0:T(8,128)(2,1)S(1)} %copy-done), kind=kOutput, calls=%fused_computation.6 | convolution fusion | flops 4294967296 | bytes 38273024 | tf_op jit(solution)/shard_map/dot_general | solution.py:9
  22.3 1.4 fusion
  23.8 58.9 %all-reduce.4.cloned.1.call-done = f32[1024,128]{1,0:T(8,128)} async-done(((f32[1024,128]{1,0:T(8,128)}), f32[1024,128]{1,0:T(8,128)}) %all-reduce.4.cloned.1.call-update) | async-done | bytes 524304 | tf_op jit(solution)/shard_map/psum | solution.py:30
  82.7 2.8 fusion.13
  85.8 40.5 %all-reduce.6.cloned.1.call-done = f32[128,128]{0,1:T(8,128)} async-done(((f32[128,128]{0,1:T(8,128)}), f32[128,128]{0,1:T(8,128)}) %all-reduce.6.cloned.1.call-update) | async-done | bytes 65552 | tf_op jit(solution)/shard_map/psum | solution.py:32
  126.3 0.9 copy.6
  127.2 0.9 fusion.10
  128.1 11.7 %cholesky.44 = f32[128,128]{1,0:T(8,128)S(1)} custom-call(f32[128,128]{1,0:T(8,128)S(1)} %fusion.10), custom_call_target="Cholesky" | custom-call | tf_op jit(solution)/shard_map/jit(cholesky)/cholesky | solution.py:23
  139.8 0.6 compare_reduce_fusion.1
  140.5 0.7 fusion.5
  141.2 9.8 %custom-call.6 = f32[1,128,128]{1,2,0:T(8,128)S(1)} custom-call(f32[1,128,128]{2,1,0:T(8,128)S(1)} %fusion.5), custom_call_target="InvertDiagBlocksLowerTriangular" | custom-call | tf_op jit(solution)/shard_map/jit(_solve_triangular)/triangular_solve | solution.py:24
  151.0 1.7 fusion.1
  152.7 1.2 fusion.14
  154.0 30.1 %copy.13 = bf16[128,8,8,2048]{3,1,2,0:T(8,128)(2,1)} copy(bf16[128,8,8,2048]{3,2,1,0:T(8,128)(2,1)} %bitcast.37) | data formatting | bytes 67108864
  184.0 11.5 %all-reduce.8.cloned.1.call-done = f32[128,128]{0,1:T(8,128)} async-done(((f32[128,128]{0,1:T(8,128)}), f32[128,128]{0,1:T(8,128)}) %all-reduce.8.cloned.1.call-update) | async-done | bytes 65552 | tf_op jit(solution)/shard_map/psum | solution.py:32
  195.6 0.9 copy.8
  196.5 0.9 fusion.8
  197.3 11.7 %cholesky.55 = f32[128,128]{1,0:T(8,128)S(1)} custom-call(f32[128,128]{1,0:T(8,128)S(1)} %fusion.8), custom_call_target="Cholesky" | custom-call | tf_op jit(solution)/shard_map/jit(cholesky)/cholesky | solution.py:23
  209.7 0.7 fusion.6
  210.4 9.8 %custom-call.7 = f32[1,128,128]{1,2,0:T(8,128)S(1)} custom-call(f32[1,128,128]{2,1,0:T(8,128)S(1)} %fusion.6), custom_call_target="InvertDiagBlocksLowerTriangular" | custom-call | tf_op jit(solution)/shard_map/jit(_solve_triangular)/triangular_solve | solution.py:24
  220.9 17.2 %convolution_convert_fusion = bf16[128,16384]{1,0:T(8,128)(2,1)} fusion(bf16[128,1024]{1,0:T(8,128)(2,1)S(1)} %convolution_convert_fusion.1, bf16[1024,16384]{1,0:T(8,128)(2,1)} %bitcast.38), kind=kOutput, calls=%fused_computation | convolution fusion | flops 4297064448 | bytes 38010880 | tf_op jit(solution)/shard_map/dot_general | solution.py:39
  238.1 52.9 %reduce-scatter.2.cloned.1.call-done = bf16[32,16384]{1,0:T(8,128)(2,1)} async-done(((bf16[128,16384]{1,0:T(8,128)(2,1)}), bf16[32,16384]{1,0:T(8,128)(2,1)}) %reduce-scatter.2.cloned.1.call-update) | async-done | bytes 1048592 | tf_op jit(solution)/shard_map/reduce_scatter | solution.py:38
  290.9 3.2 %copy.14 = f32[4,8,8,2048]{3,2,1,0:T(8,128)} copy(bf16[4,8,8,2048]{3,1,2,0:T(8,128)(2,1)} %bitcast.39) | data formatting | bytes 3145728
  (16 shorter events, 2.0 us)
Async XLA Ops:
  6.5 1.1 copy-start
  6.5 76.2 %all-reduce.4.cloned.1.call-start = ((), (), s32[]{:S(2)}) async-start(), calls=%async_computation.1 | async-start | bytes 1048576 | tf_op jit(solution)/shard_map/psum | solution.py:30
  23.7 102.6 %all-reduce.6.cloned.1.call-start = ((), (), s32[]{:S(2)}) async-start(), calls=%async_computation.2 | async-start | bytes 131072 | tf_op jit(solution)/shard_map/psum | solution.py:32
  85.6 110.0 %all-reduce.8.cloned.1.call-start = ((), (), s32[]{:S(2)}) async-start(), calls=%async_computation.3 | async-start | bytes 131072 | tf_op jit(solution)/shard_map/psum | solution.py:32
  153.9 137.0 %reduce-scatter.2.cloned.1.call-start = ((), (), s32[]{:S(2)}) async-start(), calls=%async_computation.4 | async-start | bytes 5242880 | tf_op jit(solution)/shard_map/reduce_scatter | solution.py:38
  220.8 73.3 %copy-start.1 = (bf16[2048,128]{1,0:T(8,128)(2,1)S(1)}, bf16[2048,128]{1,0:T(8,128)(2,1)}, u32[]{:S(2)}) copy-start(bf16[2048,128]{1,0:T(8,128)(2,1)} %param.7) | copy-start | bytes 1572868
Sparse Core Ops, SparseCore 0:
  23.8 58.8 all-reduce.3
  85.8 40.4 all-reduce.5
  154.0 41.4 all-reduce.7
  238.2 52.6 reduce-scatter.1
where the time goes:
time: 301 us
  waiting for transfers between devices  164 us (54%)
  other arithmetic  49.5 us (16%)
  matrix products  38.2 us (13%)
  local copies, waits for them, and re-layouts  35.4 us (12%)
  between operations  13.2 us (4%)
    psum x1, waiting for transfers between devices, shards(): basis = lax.psum(partial_value, ('ja', 'ka'))  58.9 us
    reduce_scatter x1, waiting for transfers between devices, shards(): lax.psum_scatter(lax.dot_general(basis_half, flattened, (((0,), (0,)), ((...  52.9 us
    psum x2, waiting for transfers between devices, shards(): gram = lax.psum(local_gram(basis), 'ia')  52.1 us
    unnamed x6, local copies, waits for them, and re-layouts  33.5 us
    another operation x6, other arithmetic, apply_factor(): lower = jnp.linalg.cholesky(gram)  24.8 us
    another operation x4, other arithmetic, apply_factor(): return jax.scipy.linalg.solve_triangular(lower, basis.T, lower=True).T  20.9 us
    dot_general x1, matrix products, shards(): lax.dot_general(basis_half, flattened, (((0,), (0,)), ((), ())), preferre...  17.2 us
    dot_general x1, matrix products, local_sketch(): jnp.dot(tensor.reshape(rows * slices, columns), factor_j, preferred_eleme...  14.7 us
  transfers between devices with their start and end apart: 4, of which 4 were waited for; matrix products, arithmetic and copies ran while one was open for 10% of the time, Pallas kernels for 0%

commit v1 on v0

--- a/solution.py
+++ b/solution.py
@@ -2,6 +2,7 @@
 import jax.numpy as jnp
 from jax import lax
 from jax.sharding import PartitionSpec as P
+from jax.lax import psum
 
 
 def local_sketch(tensor, factor_j, factor_k):
@@ -27,7 +28,9 @@
 def shards(tensor, factor_j, factor_k):
     rows, slices, columns = tensor.shape
     partial_value = local_sketch(tensor, factor_j, factor_k)
-    basis = lax.psum(partial_value, ("ja", "ka"))
+    basis = partial_value
+    for at in ("ka", "ja"):
+        basis = psum(basis, at)
     for sweep in range(2):
         gram = lax.psum(local_gram(basis), "ia")
         basis = apply_factor(gram, basis)

time: 301 us -> 307 us (1.020)
  waiting for transfers between devices: 164 us -> 169 us
    psum x1 -> x2, waiting for transfers between devices: 58.9 us -> 62.1 us  [shards(): basis = psum(basis, at)]
  transfers between devices with their start and end apart: 4 -> 5, of which waited for: 4 -> 5; matrix products, arithmetic and copies ran while one was open for 10% -> 10% of each run, Pallas kernels for 0% -> 0%
where the time goes in v1:
time: 307 us; the launch traced here: 306 us
  waiting for transfers between devices  169 us (55%)
  other arithmetic  49.5 us (16%)
  matrix products  38.2 us (12%)
  local copies, waits for them, and re-layouts  35.4 us (12%)
  between operations  13.2 us (4%)
    psum x2, waiting for transfers between devices, shards(): basis = psum(basis, at)  62.1 us
    psum x2, waiting for transfers between devices, shards(): gram = lax.psum(local_gram(basis), 'ia')  54.3 us
    reduce_scatter x1, waiting for transfers between devices, shards(): lax.psum_scatter(lax.dot_general(basis_half, flattened, (((0,), (0,)), ((...  52.9 us
    unnamed x6, local copies, waits for them, and re-layouts  33.5 us
    another operation x6, other arithmetic, apply_factor(): lower = jnp.linalg.cholesky(gram)  24.8 us
    another operation x4, other arithmetic, apply_factor(): return jax.scipy.linalg.solve_triangular(lower, basis.T, lower=True).T  20.9 us
    dot_general x1, matrix products, shards(): lax.dot_general(basis_half, flattened, (((0,), (0,)), ((), ())), preferre...  17.2 us
    dot_general x1, matrix products, local_sketch(): jnp.dot(tensor.reshape(rows * slices, columns), factor_j, preferred_eleme...  14.7 us
  transfers between devices with their start and end apart: 5, of which 5 were waited for; matrix products, arithmetic and copies ran while one was open for 10% of the time, Pallas kernels for 0%

profile of v1, /device:TPU:0, one launch (start us, length us, event | category | flops | bytes accessed | tf_op | source)
XLA Modules:
  0.0 306.1 jit_solution(3137798809151796645)
XLA Ops:
  6.5 0.7 convert_element_type.11
  7.6 14.7 %fusion.3 = f32[1024,8,128]{2,1,0:T(8,128)S(1)} fusion(bf16[1024,8,2048]{2,1,0:T(8,128)(2,1)} %param.6, bf16[2048,128]{1,0:T(8,128)(2,1)S(1)} %copy-done), kind=kOutput, calls=%fused_computation.6 | convolution fusion | flops 4294967296 | bytes 38273024 | tf_op jit(solution)/shard_map/dot_general | solution.py:10
  22.3 1.4 fusion
  23.8 41.1 %all-reduce.5.cloned.1.call-done = f32[1024,128]{1,0:T(8,128)} async-done(((f32[1024,128]{1,0:T(8,128)}), f32[1024,128]{1,0:T(8,128)}) %all-reduce.5.cloned.1.call-update) | async-done | bytes 524304 | tf_op jit(solution)/shard_map/psum | solution.py:33
  64.9 21.0 %all-reduce.7.cloned.1.call-done = f32[1024,128]{1,0:T(8,128)} async-done(((f32[1024,128]{1,0:T(8,128)}), f32[1024,128]{1,0:T(8,128)}) %all-reduce.7.cloned.1.call-update) | async-done | bytes 524304 | tf_op jit(solution)/shard_map/psum | solution.py:33
  85.9 2.8 fusion.13
  89.0 42.7 %all-reduce.9.cloned.1.call-done = f32[128,128]{0,1:T(8,128)} async-done(((f32[128,128]{0,1:T(8,128)}), f32[128,128]{0,1:T(8,128)}) %all-reduce.9.cloned.1.call-update) | async-done | bytes 65552 | tf_op jit(solution)/shard_map/psum | solution.py:35
  131.7 0.9 copy.6
  132.7 0.9 fusion.10
  133.5 11.7 %cholesky.44 = f32[128,128]{1,0:T(8,128)S(1)} custom-call(f32[128,128]{1,0:T(8,128)S(1)} %fusion.10), custom_call_target="Cholesky" | custom-call | tf_op jit(solution)/shard_map/jit(cholesky)/cholesky | solution.py:24
  145.9 0.7 fusion.5
  146.6 9.8 %custom-call.6 = f32[1,128,128]{1,2,0:T(8,128)S(1)} custom-call(f32[1,128,128]{2,1,0:T(8,128)S(1)} %fusion.5), custom_call_target="InvertDiagBlocksLowerTriangular" | custom-call | tf_op jit(solution)/shard_map/jit(_solve_triangular)/triangular_solve | solution.py:25
  156.4 1.7 fusion.1
  158.1 1.2 fusion.14
  159.4 30.1 %copy.13 = bf16[128,8,8,2048]{3,1,2,0:T(8,128)(2,1)} copy(bf16[128,8,8,2048]{3,2,1,0:T(8,128)(2,1)} %bitcast.37) | data formatting | bytes 67108864
  189.4 11.6 %all-reduce.11.cloned.1.call-done = f32[128,128]{0,1:T(8,128)} async-done(((f32[128,128]{0,1:T(8,128)}), f32[128,128]{0,1:T(8,128)}) %all-reduce.11.cloned.1.call-update) | async-done | bytes 65552 | tf_op jit(solution)/shard_map/psum | solution.py:35
  201.0 0.9 copy.8
  201.9 0.9 fusion.8
  202.8 11.7 %cholesky.55 = f32[128,128]{1,0:T(8,128)S(1)} custom-call(f32[128,128]{1,0:T(8,128)S(1)} %fusion.8), custom_call_target="Cholesky" | custom-call | tf_op jit(solution)/shard_map/jit(cholesky)/cholesky | solution.py:24
  215.2 0.7 fusion.6
  215.8 9.8 %custom-call.7 = f32[1,128,128]{1,2,0:T(8,128)S(1)} custom-call(f32[1,128,128]{2,1,0:T(8,128)S(1)} %fusion.6), custom_call_target="InvertDiagBlocksLowerTriangular" | custom-call | tf_op jit(solution)/shard_map/jit(_solve_triangular)/triangular_solve | solution.py:25
  226.3 17.2 %convolution_convert_fusion = bf16[128,16384]{1,0:T(8,128)(2,1)} fusion(bf16[128,1024]{1,0:T(8,128)(2,1)S(1)} %convolution_convert_fusion.1, bf16[1024,16384]{1,0:T(8,128)(2,1)} %bitcast.38), kind=kOutput, calls=%fused_computation | convolution fusion | flops 4297064448 | bytes 38010880 | tf_op jit(solution)/shard_map/dot_general | solution.py:42
  243.5 52.9 %reduce-scatter.2.cloned.1.call-done = bf16[32,16384]{1,0:T(8,128)(2,1)} async-done(((bf16[128,16384]{1,0:T(8,128)(2,1)}), bf16[32,16384]{1,0:T(8,128)(2,1)}) %reduce-scatter.2.cloned.1.call-update) | async-done | bytes 1048592 | tf_op jit(solution)/shard_map/reduce_scatter | solution.py:41
  296.4 3.2 %copy.14 = f32[4,8,8,2048]{3,2,1,0:T(8,128)} copy(bf16[4,8,8,2048]{3,1,2,0:T(8,128)(2,1)} %bitcast.39) | data formatting | bytes 3145728
  (19 shorter events, 2.7 us)
Async XLA Ops:
  6.5 1.1 copy-start
  6.5 58.3 %all-reduce.5.cloned.1.call-start = ((), (), s32[]{:S(2)}) async-start(), calls=%async_computation.1 | async-start | bytes 1048576 | tf_op jit(solution)/shard_map/psum | solution.py:33
  23.7 62.2 %all-reduce.7.cloned.1.call-start = ((), (), s32[]{:S(2)}) async-start(), calls=%async_computation.2 | async-start | bytes 1048576 | tf_op jit(solution)/shard_map/psum | solution.py:33
  64.9 66.9 %all-reduce.9.cloned.1.call-start = ((), (), s32[]{:S(2)}) async-start(), calls=%async_computation.3 | async-start | bytes 131072 | tf_op jit(solution)/shard_map/psum | solution.py:35
  88.8 112.2 %all-reduce.11.cloned.1.call-start = ((), (), s32[]{:S(2)}) async-start(), calls=%async_computation.4 | async-start | bytes 131072 | tf_op jit(solution)/shard_map/psum | solution.py:35
  159.3 137.0 %reduce-scatter.2.cloned.1.call-start = ((), (), s32[]{:S(2)}) async-start(), calls=%async_computation.5 | async-start | bytes 5242880 | tf_op jit(solution)/shard_map/reduce_scatter | solution.py:41
  226.3 73.2 %copy-start.1 = (bf16[2048,128]{1,0:T(8,128)(2,1)S(1)}, bf16[2048,128]{1,0:T(8,128)(2,1)}, u32[]{:S(2)}) copy-start(bf16[2048,128]{1,0:T(8,128)(2,1)} %param.7) | copy-start | bytes 1572868
Sparse Core Ops, SparseCore 0:
  23.8 40.9 all-reduce.4
  67.2 18.6 all-reduce.6
  89.0 42.6 all-reduce.8
  159.4 41.4 all-reduce.10
  243.6 52.6 reduce-scatter.1

commit v2 on v0

--- a/solution.py
+++ b/solution.py
@@ -2,6 +2,10 @@
 import jax.numpy as jnp
 from jax import lax
 from jax.sharding import PartitionSpec as P
+
+
+def get_view(panel, axis_name):
+    return jax.lax.all_gather(panel, axis_name).sum(axis=0)
 
 
 def local_sketch(tensor, factor_j, factor_k):
@@ -29,7 +33,7 @@
     partial_value = local_sketch(tensor, factor_j, factor_k)
     basis = lax.psum(partial_value, ("ja", "ka"))
     for sweep in range(2):
-        gram = lax.psum(local_gram(basis), "ia")
+        gram = get_view(local_gram(basis), "ia")
         basis = apply_factor(gram, basis)
     basis_half = basis.astype(jnp.bfloat16)
     flattened = tensor.reshape(rows, slices * columns)

time: 301 us -> 231 us (0.77)
  waiting for transfers between devices: 164 us -> 80.2 us
  blocking collectives: 0 us -> 18.3 us
    psum x2 -> x0, waiting for transfers between devices: 52.1 us -> none  [shards(): gram = lax.psum(local_gram(basis), 'ia')]
    psum x1, waiting for transfers between devices: 58.9 us -> 28.9 us  [shards(): basis = lax.psum(partial_value, ('ja', 'ka'))]
    all_gather x0 -> x2, blocking collectives: none -> 18.3 us  [get_view(): return jax.lax.all_gather(panel, axis_name).sum(axis=0)]
  transfers between devices with their start and end apart: 4 -> 2, of which waited for: 4 -> 2; matrix products, arithmetic and copies ran while one was open for 10% -> 13% of each run, Pallas kernels for 0% -> 0%
where the time goes in v2:
time: 231 us
  waiting for transfers between devices  80.2 us (35%)
  other arithmetic  47.9 us (21%)
  matrix products  37 us (16%)
  local copies, waits for them, and re-layouts  33.7 us (15%)
  blocking collectives  18.3 us (8%)
  between operations  13.5 us (6%)
    reduce_scatter x1, waiting for transfers between devices, shards(): lax.psum_scatter(lax.dot_general(basis_half, flattened, (((0,), (0,)), ((...  51.2 us
    unnamed x6, local copies, waits for them, and re-layouts  33.5 us
    psum x1, waiting for transfers between devices, shards(): basis = lax.psum(partial_value, ('ja', 'ka'))  28.9 us
    another operation x6, other arithmetic, apply_factor(): lower = jnp.linalg.cholesky(gram)  24.8 us
    another operation x4, other arithmetic, apply_factor(): return jax.scipy.linalg.solve_triangular(lower, basis.T, lower=True).T  20.9 us
    all_gather x2, blocking collectives, get_view(): return jax.lax.all_gather(panel, axis_name).sum(axis=0)  18.3 us
    dot_general x1, matrix products, shards(): lax.dot_general(basis_half, flattened, (((0,), (0,)), ((), ())), preferre...  17.2 us
    dot_general x1, matrix products, local_sketch(): jnp.dot(tensor.reshape(rows * slices, columns), factor_j, preferred_eleme...  14.7 us
  transfers between devices with their start and end apart: 2, of which 2 were waited for; matrix products, arithmetic and copies ran while one was open for 13% of the time, Pallas kernels for 0%

profile of v2, /device:TPU:0, one launch (start us, length us, event | category | flops | bytes accessed | tf_op | source)
XLA Modules:
  0.0 230.6 jit_solution(17668241740844972866)
XLA Ops:
  6.5 0.7 convert_element_type.11
  7.3 0.3 copy-done
  7.6 14.7 %fusion.3 = f32[1024,8,128]{2,1,0:T(8,128)S(1)} fusion(bf16[1024,8,2048]{2,1,0:T(8,128)(2,1)} %param.6, bf16[2048,128]{1,0:T(8,128)(2,1)S(1)} %copy-done), kind=kOutput, calls=%fused_computation.6 | convolution fusion | flops 4294967296 | bytes 38273024 | tf_op jit(solution)/shard_map/dot_general | solution.py:13
  22.3 1.4 fusion
  23.8 30.1 %copy.12 = bf16[128,8,8,2048]{3,1,2,0:T(8,128)(2,1)} copy(bf16[128,8,8,2048]{3,2,1,0:T(8,128)(2,1)} %bitcast.39) | data formatting | bytes 67108864
  53.8 28.9 %all-reduce.2.cloned.1.call-done = f32[1024,128]{1,0:T(8,128)} async-done(((f32[1024,128]{1,0:T(8,128)}), f32[1024,128]{1,0:T(8,128)}) %all-reduce.2.cloned.1.call-update) | async-done | bytes 524304 | tf_op jit(solution)/shard_map/psum | solution.py:34
  82.7 2.2 fusion.13
  84.9 9.4 %all-gather = f32[512,128]{1,0:T(8,128)S(1)} all-gather(f32[128,128]{1,0:T(8,128)S(1)} %fusion.13), channel_id=2, replica_groups=mesh['ia'=4,'ja'=2,'ka'=4] {'ia'}, dimensions={0}, use_global_device_ids=true | all-gather | bytes 327680 | tf_op jit(solution)/shard_map/all_gather | solution.py:8
  94.4 0.1 copy.8
  94.5 11.7 %cholesky.44 = f32[128,128]{1,0:T(8,128)S(1)} custom-call(f32[128,128]{1,0:T(8,128)S(1)} %fusion.10), custom_call_target="Cholesky" | custom-call | tf_op jit(solution)/shard_map/jit(cholesky)/cholesky | solution.py:27
  106.2 0.6 compare_reduce_fusion.1
  106.9 0.7 fusion.5
  107.5 9.8 %custom-call.6 = f32[1,128,128]{1,2,0:T(8,128)S(1)} custom-call(f32[1,128,128]{2,1,0:T(8,128)S(1)} %fusion.5), custom_call_target="InvertDiagBlocksLowerTriangular" | custom-call | tf_op jit(solution)/shard_map/jit(_solve_triangular)/triangular_solve | solution.py:28
  117.3 1.7 fusion.1
  119.0 0.6 fusion.14
  119.6 8.9 %all-gather.1 = f32[512,128]{1,0:T(8,128)S(1)} all-gather(f32[128,128]{1,0:T(8,128)S(1)} %fusion.14), channel_id=3, replica_groups=mesh['ia'=4,'ja'=2,'ka'=4] {'ia'}, dimensions={0}, use_global_device_ids=true | all-gather | bytes 327680 | tf_op jit(solution)/shard_map/all_gather | solution.py:8
  128.7 11.7 %cholesky.55 = f32[128,128]{1,0:T(8,128)S(1)} custom-call(f32[128,128]{1,0:T(8,128)S(1)} %fusion.8), custom_call_target="Cholesky" | custom-call | tf_op jit(solution)/shard_map/jit(cholesky)/cholesky | solution.py:27
  140.4 0.6 compare_reduce_fusion
  141.1 0.7 fusion.6
  141.7 9.8 %custom-call.7 = f32[1,128,128]{1,2,0:T(8,128)S(1)} custom-call(f32[1,128,128]{2,1,0:T(8,128)S(1)} %fusion.6), custom_call_target="InvertDiagBlocksLowerTriangular" | custom-call | tf_op jit(solution)/shard_map/jit(_solve_triangular)/triangular_solve | solution.py:28
  151.5 0.6 convolution_convert_fusion.1
  152.2 17.2 %convolution_convert_fusion = bf16[128,16384]{1,0:T(8,128)(2,1)} fusion(bf16[128,1024]{1,0:T(8,128)(2,1)S(1)} %convolution_convert_fusion.1, bf16[1024,16384]{1,0:T(8,128)(2,1)} %bitcast.40), kind=kOutput, calls=%fused_computation | convolution fusion | flops 4297064448 | bytes 38010880 | tf_op jit(solution)/shard_map/dot_general | solution.py:43
  169.4 51.2 %reduce-scatter.2.cloned.1.call-done = bf16[32,16384]{1,0:T(8,128)(2,1)} async-done(((bf16[128,16384]{1,0:T(8,128)(2,1)}), bf16[32,16384]{1,0:T(8,128)(2,1)}) %reduce-scatter.2.cloned.1.call-update) | async-done | bytes 1048592 | tf_op jit(solution)/shard_map/reduce_scatter | solution.py:42
  220.6 3.2 %copy.13 = f32[4,8,8,2048]{3,2,1,0:T(8,128)} copy(bf16[4,8,8,2048]{3,1,2,0:T(8,128)(2,1)} %bitcast.41) | data formatting | bytes 3145728
  (14 shorter events, 0.3 us)
Async XLA Ops:
  6.5 1.1 copy-start
  6.5 76.2 %all-reduce.2.cloned.1.call-start = ((), (), s32[]{:S(2)}) async-start(), calls=%async_computation.1 | async-start | bytes 1048576 | tf_op jit(solution)/shard_map/psum | solution.py:34
  23.7 196.9 %reduce-scatter.2.cloned.1.call-start = ((), (), s32[]{:S(2)}) async-start(), calls=%async_computation.2 | async-start | bytes 5242880 | tf_op jit(solution)/shard_map/reduce_scatter | solution.py:42
  152.2 71.6 %copy-start.1 = (bf16[2048,128]{1,0:T(8,128)(2,1)S(1)}, bf16[2048,128]{1,0:T(8,128)(2,1)}, u32[]{:S(2)}) copy-start(bf16[2048,128]{1,0:T(8,128)(2,1)} %param.7) | copy-start | bytes 1572868
Sparse Core Ops, SparseCore 0:
  23.8 58.8 all-reduce.1
  169.5 51.0 reduce-scatter.1
